TPU v7x, 256 devices: a whole 4x4x8 slice. The times are simulated.
256 devices in a mesh: ctx: 64 (over z, x, y_lo), rep: 4 (over y_hi, core).
Axes of the slice: x: 4, y: 4 (y_hi: 2, y_lo: 2; y = y_hi * 2 + y_lo), z: 8, core: 2. Of those that a mesh axis runs over, the one named last changes fastest.
Arguments:
- gated_input: bfloat16 [8, 256, 32768], P('rep', None, 'ctx'), may hold values from -6 to 6
- out_grad: bfloat16 [8, 256, 32768], P('rep', None, 'ctx'), may hold values from -6 to 6
- filter_taps: float32 [256, 32768], P('ctx'), may hold values from -1 to 1
Outputs:
- input_grad: bfloat16 [8, 256, 32768], P('rep', None, 'ctx')
- filter_grad: float32 [256, 32768], P(('ctx', 'rep'))
All inputs are finite; a program needn't handle non-finite values.
Results may differ from a plain program's by a relative error of at most 0.002.
Values may be sent and summed in bfloat16 or wider, within the bound.
A program may use at most 128 MiB of HBM per device.

v0:
```python
import functools
import math

import jax
import jax.numpy as jnp
import ml_dtypes
import numpy as np
from jax import lax
from jax.experimental import pallas as pl
from jax.experimental.pallas import tpu as pltpu
from jax.sharding import PartitionSpec as P

MESH = pl.DeviceIdType.MESH
CTX = 64
REP = 4
ROWS = 16
F32 = jnp.float32
BF16 = jnp.bfloat16

P1, P3, P2, A2, DHI, DLO, EHI, ELO, BB = range(9)


def split16(table):
    high = table.astype(ml_dtypes.bfloat16)
    low = (table - high.astype(np.float64)).astype(ml_dtypes.bfloat16)
    return high, low


def bf16_tables():
    out = np.zeros((9, 256, 256), ml_dtypes.bfloat16)
    for chan in range(64):
        for seq in range(2):
            for half in range(2):
                row = (chan // 4) * 16 + seq * 8 + (chan % 4) * 2 + half
                col = seq * 128 + half * 64 + chan
                out[P1, row, col] = 1
                out[P3, col, row] = 1
    for at in range(256):
        out[P2, (at % 16) * 16 + at // 16, at] = 1
    place = np.arange(128)
    pos = 2 * (place % 64) + place // 64
    k1 = np.arange(128)
    angle = 2 * math.pi * ((pos[None, :] * (2 * k1[:, None] + 1)) % 512) / 512
    first = np.concatenate([np.cos(angle), -np.sin(angle)], 0)
    high, low = split16(first)
    out[A2] = np.concatenate([high, low], 1)
    high, low = split16(first.T * 2.0**-15)
    out[BB] = np.concatenate([high, low], 0)
    turn = 2 * math.pi * ((k1[:, None] * k1[None, :]) % 128) / 128
    cos, sin = np.cos(turn), np.sin(turn)
    out[DHI], out[DLO] = split16(np.block([[cos, -sin], [sin, cos]]))
    out[EHI], out[ELO] = split16(np.block([[cos, sin], [-sin, cos]]))
    return out


def f32_tables():
    k1 = np.arange(128)[:, None]
    q = np.arange(256)[None, :]
    angle = 2 * math.pi * (q * (2 * k1 + 1)) / 131072
    half = np.broadcast_to(2 * math.pi * np.arange(128)[None, :] / 256, (128, 128))
    return np.concatenate(
        [np.cos(angle), -np.sin(angle), np.cos(half), -np.sin(half)], 1
    ).astype(np.float32)


def dot(left, right):
    return jnp.dot(left, right, preferred_element_type=F32)


def halves(value):
    high = value.astype(BF16)
    return high, (value - high.astype(F32)).astype(BF16)


def cmul(ar, ai, br, bi):
    return ar * br - ai * bi, ar * bi + ai * br


def forward_tail(tab, tw, step):
    t0r, t1r = tw[:, 0:128], tw[:, 128:256]
    t0i, t1i = tw[:, 256:384], tw[:, 384:512]
    wr, wi = tw[:, 512:640], tw[:, 640:768]
    z0r, z0i = cmul(step[:128, :128], step[128:, :128], t0r, t0i)
    z1r, z1i = cmul(step[:128, 128:], step[128:, 128:], t1r, t1i)
    odd_r, odd_i = cmul(z0r - z1r, z0i - z1i, wr, wi)
    both = jnp.concatenate(
        [
            jnp.concatenate([z0r + z1r, z0i + z1i], 1),
            jnp.concatenate([odd_r, odd_i], 1),
        ],
        0,
    )
    high, low = halves(both)
    return dot(high, tab[DHI]) + dot(low, tab[DHI]) + dot(high, tab[DLO])


def inverse(tab, tw, spec):
    high, low = halves(spec)
    back = dot(high, tab[EHI]) + dot(low, tab[EHI]) + dot(high, tab[ELO])
    t0r, t1r = tw[:, 0:128], tw[:, 128:256]
    t0i, t1i = tw[:, 256:384], tw[:, 384:512]
    wr, wi = tw[:, 512:640], tw[:, 640:768]
    er, ei = back[:128, :128], back[:128, 128:]
    dr, di = cmul(back[128:, :128], back[128:, 128:], wr, -wi)
    a0r, a0i = cmul(er + dr, ei + di, t0r, -t0i)
    a1r, a1i = cmul(er - dr, ei - di, t1r, -t1i)
    stack = jnp.concatenate(
        [jnp.concatenate([a0r, a1r], 1), jnp.concatenate([a0i, a1i], 1)], 0
    )
    high, low = halves(stack)
    wide = dot(tab[BB], high)
    return wide[:128] + wide[128:] + dot(tab[BB, :128, :], low)


def kernel(
    og_hbm, gi_hbm, flt_hbm, tab_hbm, tw_hbm,
    ig_out, fg_out,
    og_in, gi_in, flt, tab, tw,
    og_send, gi_send, ig_send, og_recv, gi_recv, ig_recv,
    rows, grad_spec, flt_spec, fg_part, fg_recv,
    in_sem, send_sem, recv_sem, fg_send_sem, fg_recv_sem,
):
    me = lax.axis_index("ctx")
    rep = lax.axis_index("rep")

    loads = [
        pltpu.make_async_copy(src, dst, in_sem.at[at])
        for at, (src, dst) in enumerate(
            ((og_hbm, og_in), (tab_hbm, tab), (gi_hbm, gi_in), (flt_hbm, flt), (tw_hbm, tw))
        )
    ]
    for load in loads:
        load.start()

    barrier = pltpu.get_barrier_semaphore()

    def greet(step, _):
        pl.semaphore_signal(
            barrier, inc=1, device_id={"ctx": lax.rem(me + step, CTX)}, device_id_type=MESH
        )
        return 0

    lax.fori_loop(1, CTX, greet, 0)
    for step in range(1, REP):
        pl.semaphore_signal(
            barrier, inc=1, device_id={"rep": lax.rem(rep + step, REP)}, device_id_type=MESH
        )

    def arrange(source, target):
        def group(at, _):
            chans = pl.ds(pl.multiple_of(at * 64, 64), 64)
            block = jnp.concatenate(
                [
                    source[seq, chans, half * 256 : half * 256 + 256]
                    for seq in range(2)
                    for half in range(2)
                ],
                0,
            )
            target[pl.ds(pl.multiple_of(at * 256, 256), 256), :] = dot(tab[P1], block).astype(BF16)
            return 0

        lax.fori_loop(0, 4, group, 0)

    mine = pl.ds(pl.multiple_of(me * ROWS, ROWS), ROWS)

    def send_all(source, target, which):
        def send(step, _):
            to = lax.rem(me + step, CTX)
            pltpu.make_async_remote_copy(
                src_ref=source.at[pl.ds(pl.multiple_of(to * ROWS, ROWS), ROWS), :],
                dst_ref=target.at[mine, :],
                send_sem=send_sem.at[which],
                recv_sem=recv_sem.at[which],
                device_id={"ctx": to},
                device_id_type=MESH,
            ).start()
            return 0

        lax.fori_loop(1, CTX, send, 0)
        target[mine, :] = source[mine, :]

    def wait_all(buffer, sems, which):
        part = buffer.at[pl.ds(0, (CTX - 1) * ROWS), :]
        pltpu.make_async_copy(part, part, sems.at[which]).wait()

    loads[0].wait()
    loads[1].wait()
    arrange(og_in, og_send)
    pl.semaphore_wait(barrier, CTX - 1 + REP - 1)
    send_all(og_send, og_recv, 0)
    loads[2].wait()
    arrange(gi_in, gi_send)
    send_all(gi_send, gi_recv, 1)
    loads[3].wait()
    loads[4].wait()

    def filter_spectrum(chan, _):
        taps = jnp.concatenate(
            [
                jnp.concatenate(
                    [flt[pl.ds(8 * half + 4 * high + chan, 64, stride=16), :] for high in range(2)], 1
                )
                for half in range(2)
            ],
            0,
        )
        high, low = halves(taps)
        step = dot(tab[A2], jnp.concatenate([high, high], 0)) + dot(tab[A2, :, :128], low)
        flt_spec[chan] = forward_tail(tab, tw, step)
        return 0

    lax.fori_loop(0, 4, filter_spectrum, 0)

    def to_rows(buffer):
        def group(at, _):
            block = buffer[pl.ds(pl.multiple_of(at * 256, 256), 256), :]
            turned = dot(tab[P2], block).astype(BF16)
            for row in range(16):
                rows[pl.ds(pl.multiple_of(row * 64 + at * 16, 16), 16), :] = turned[row * 16 : row * 16 + 16]
            return 0

        lax.fori_loop(0, 4, group, 0)

    def spectrum(at):
        block = rows[pl.ds(pl.multiple_of(at * 128, 128), 128), :]
        return forward_tail(tab, tw, dot(tab[A2], jnp.concatenate([block, block], 0)))

    wait_all(og_recv, recv_sem, 0)
    to_rows(og_recv)

    def input_grad(at, _):
        spec = spectrum(at)
        grad_spec[at] = spec
        taps = flt_spec[lax.rem(at, 4)]
        sr, si, fr, fi = spec[:, :128], spec[:, 128:], taps[:, :128], taps[:, 128:]
        corr = jnp.concatenate([fr * sr + fi * si, fr * si - fi * sr], 1)
        rows[pl.ds(pl.multiple_of(at * 128, 128), 128), :] = inverse(tab, tw, corr).astype(BF16)
        return 0

    lax.fori_loop(0, 8, input_grad, 0)

    def from_rows(at, _):
        block = jnp.concatenate(
            [rows[pl.ds(pl.multiple_of(row * 64 + at * 16, 16), 16), :] for row in range(16)], 0
        )
        ig_send[pl.ds(pl.multiple_of(at * 256, 256), 256), :] = dot(tab[P2], block).astype(BF16)
        return 0

    lax.fori_loop(0, 4, from_rows, 0)
    send_all(ig_send, ig_recv, 2)

    wait_all(gi_recv, recv_sem, 1)
    to_rows(gi_recv)

    def filter_grad(chan, _):
        total_r = total_i = None
        for seq in range(2):
            at = chan + 4 * seq
            spec = spectrum(at)
            grad = grad_spec[at]
            sr, si, gr, gi = spec[:, :128], spec[:, 128:], grad[:, :128], grad[:, 128:]
            real, imag = sr * gr + si * gi, sr * gi - si * gr
            total_r = real if total_r is None else total_r + real
            total_i = imag if total_i is None else total_i + imag
        fg_part[chan] = inverse(tab, tw, jnp.concatenate([total_r, total_i], 1))
        return 0

    lax.fori_loop(0, 4, filter_grad, 0)

    for step in range(1, REP):
        to = lax.rem(rep + step, REP)
        pltpu.make_async_remote_copy(
            src_ref=fg_part.at[to],
            dst_ref=fg_recv.at[step - 1],
            send_sem=fg_send_sem.at[step - 1],
            recv_sem=fg_recv_sem.at[step - 1],
            device_id={"rep": to},
            device_id_type=MESH,
        ).start()
    total = fg_part[rep]
    for step in range(1, REP):
        slot = fg_recv.at[step - 1]
        pltpu.make_async_copy(slot, slot, fg_recv_sem.at[step - 1]).wait()
        total = total + fg_recv[step - 1]
    total = total * (1.0 / 512.0)
    for half in range(2):
        for high in range(2):
            fg_out[pl.ds(2 * half + high, 64, stride=4), :] = total[
                half * 64 : half * 64 + 64, high * 128 : high * 128 + 128
            ]

    wait_all(ig_recv, recv_sem, 2)

    def finish(at, _):
        block = ig_recv[pl.ds(pl.multiple_of(at * 256, 256), 256), :]
        turned = dot(tab[P3], block).astype(BF16)
        chans = pl.ds(pl.multiple_of(at * 64, 64), 64)
        for seq in range(2):
            for half in range(2):
                start = seq * 128 + half * 64
                ig_out[seq, chans, half * 256 : half * 256 + 256] = turned[start : start + 64]
        return 0

    lax.fori_loop(0, 4, finish, 0)
    wait_all(og_send, send_sem, 0)
    wait_all(gi_send, send_sem, 1)
    wait_all(ig_send, send_sem, 2)
    for step in range(1, REP):
        slot = fg_part.at[step - 1]
        pltpu.make_async_copy(slot, slot, fg_send_sem.at[step - 1]).wait()


def local(gated_input, out_grad, filter_taps):
    taps = filter_taps.reshape(4, 256, 128).transpose(1, 0, 2).reshape(1024, 128)
    any_spec = pl.BlockSpec(memory_space=pl.ANY)
    vmem = pl.BlockSpec(memory_space=pltpu.VMEM)
    chunks = pltpu.VMEM((CTX * ROWS, 256), BF16)
    input_grad, filter_grad = pl.pallas_call(
        kernel,
        out_shape=(
            jax.ShapeDtypeStruct((2, 256, 512), BF16),
            jax.ShapeDtypeStruct((256, 128), F32),
        ),
        in_specs=[any_spec] * 5,
        out_specs=(vmem, vmem),
        scratch_shapes=[
            pltpu.VMEM((2, 256, 512), BF16),
            pltpu.VMEM((2, 256, 512), BF16),
            pltpu.VMEM((1024, 128), F32),
            pltpu.VMEM((9, 256, 256), BF16),
            pltpu.VMEM((128, 768), F32),
            chunks, chunks, chunks, chunks, chunks, chunks,
            chunks,
            pltpu.VMEM((8, 256, 256), F32),
            pltpu.VMEM((4, 256, 256), F32),
            pltpu.VMEM((4, 128, 256), F32),
            pltpu.VMEM((3, 128, 256), F32),
            pltpu.SemaphoreType.DMA((5,)),
            pltpu.SemaphoreType.DMA((3,)),
            pltpu.SemaphoreType.DMA((3,)),
            pltpu.SemaphoreType.DMA((3,)),
            pltpu.SemaphoreType.DMA((3,)),
        ],
        compiler_params=pltpu.CompilerParams(
            collective_id=0, has_side_effects=True, vmem_limit_bytes=48 * 2**20
        ),
    )(out_grad, gated_input, taps, jnp.asarray(bf16_tables()), jnp.asarray(f32_tables()))
    return input_grad, filter_grad.reshape(1, 32768)


def solution(mesh):
    return jax.shard_map(
        local,
        mesh=mesh,
        in_specs=(P("rep", None, "ctx"), P("rep", None, "ctx"), P("ctx", None)),
        out_specs=(P("rep", None, "ctx"), P(("ctx", "rep"), None)),
        check_vma=False,
    )
```

profile of v0, /device:TPU:1, one launch (start us, length us, event | category | flops | bytes accessed | tf_op | source)
XLA Modules:
  0.0 60.8 jit_solution(8737255507511099830)
XLA Ops:
  0.6 0.0 copy-start
  0.6 1.3 %copy-done = bf16[9,256,256]{2,1,0:T(8,128)(2,1)S(1)} copy-done((bf16[9,256,256]{2,1,0:T(8,128)(2,1)S(1)}, bf16[9,256,256]{2,1,0:T(8,128)(2,1)}, u32[]{:S(2)}) %copy-start) | copy-done | bytes 1179672
  1.9 0.0 copy-start.1
  1.9 1.0 %copy-done.1 = bf16[2,256,512]{2,1,0:T(8,128)(2,1)S(1)} copy-done((bf16[2,256,512]{2,1,0:T(8,128)(2,1)S(1)}, bf16[2,256,512]{2,1,0:T(8,128)(2,1)}, u32[]{:S(2)}) %copy-start.1) | copy-done | bytes 524312
  2.9 0.0 copy-start.2
  2.9 1.0 %copy-done.2 = bf16[2,256,512]{2,1,0:T(8,128)(2,1)S(1)} copy-done((bf16[2,256,512]{2,1,0:T(8,128)(2,1)S(1)}, bf16[2,256,512]{2,1,0:T(8,128)(2,1)}, u32[]{:S(2)}) %copy-start.2) | copy-done | bytes 524312
  4.0 0.0 copy-start.3
  4.0 1.0 %copy-done.3 = f32[4,32768]{1,0:T(4,128)S(1)} copy-done((f32[4,32768]{1,0:T(4,128)S(1)}, f32[4,32768]{1,0:T(4,128)}, u32[]{:S(2)}) %copy-start.3) | copy-done | bytes 524312
  5.0 0.0 copy-start.4
  5.0 1.0 %copy-done.4 = f32[128,768]{1,0:T(8,128)S(1)} copy-done((f32[128,768]{1,0:T(8,128)S(1)}, f32[128,768]{1,0:T(8,128)}, u32[]{:S(2)}) %copy-start.4) | copy-done | bytes 393240
  6.0 53.3 %shard_map.68 = (bf16[2,256,512]{2,1,0:T(8,128)(2,1)S(1)}, f32[256,128]{1,0:T(8,128)S(1)}) custom-call(bf16[2,256,512]{2,1,0:T(8,128)(2,1)S(1)} %copy-done.1, bf16[2,256,512]{2,1,0:T(8,128)(2,1)S(1)} %copy-done.2, f32[1024,128]{1,0:T(8,128)S(1)} %bitcast.6, bf16[9,256,256]{2,1,0:T(8,128)(2,1)S(1)} %copy-done, f32[128,768]{1,0:T(8,128)S(1)} %copy-done.4), custom_call_target="tpu_custom_call" | custom-call | tf_op jit(solution)/shard_map/pallas_call | solution.py:319
  59.3 0.8 %copy.10 = bf16[2,256,512]{2,1,0:T(8,128)(2,1)} copy(bf16[2,256,512]{2,1,0:T(8,128)(2,1)S(1)} %get-tuple-element.8) | data formatting | bytes 1048576
  60.1 0.7 %copy.11 = f32[1,32768]{1,0:T(1,128)} copy(f32[1,32768]{1,0:T(1,128)S(1)} %bitcast.7) | data formatting | bytes 262144
Async XLA Ops:
  0.6 1.3 %copy-start = (bf16[9,256,256]{2,1,0:T(8,128)(2,1)S(1)}, bf16[9,256,256]{2,1,0:T(8,128)(2,1)}, u32[]{:S(2)}) copy-start(bf16[9,256,256]{2,1,0:T(8,128)(2,1)} %constant.4.clone.tab_hbm) | copy-start | bytes 3538948
  1.9 1.0 %copy-start.1 = (bf16[2,256,512]{2,1,0:T(8,128)(2,1)S(1)}, bf16[2,256,512]{2,1,0:T(8,128)(2,1)}, u32[]{:S(2)}) copy-start(bf16[2,256,512]{2,1,0:T(8,128)(2,1)} %og_hbm.1) | copy-start | bytes 1572868
  2.9 1.0 %copy-start.2 = (bf16[2,256,512]{2,1,0:T(8,128)(2,1)S(1)}, bf16[2,256,512]{2,1,0:T(8,128)(2,1)}, u32[]{:S(2)}) copy-start(bf16[2,256,512]{2,1,0:T(8,128)(2,1)} %gi_hbm.1) | copy-start | bytes 1572868
  4.0 1.0 %copy-start.3 = (f32[4,32768]{1,0:T(4,128)S(1)}, f32[4,32768]{1,0:T(4,128)}, u32[]{:S(2)}) copy-start(f32[4,32768]{1,0:T(4,128)} %param.7) | copy-start | bytes 1572868
  5.0 1.0 %copy-start.4 = (f32[128,768]{1,0:T(8,128)S(1)}, f32[128,768]{1,0:T(8,128)}, u32[]{:S(2)}) copy-start(f32[128,768]{1,0:T(8,128)} %constant.5.clone.tw_hbm) | copy-start | bytes 1179652
where the time goes:
time: 61.4 us; the launch traced here: 60.8 us
  Pallas kernels  53.3 us (87%)
  local copies, waits for them, and re-layouts  6.84 us (11%)
  between operations  0.65 us (1%)
    pallas_call x1, Pallas kernels, local(): pl.pallas_call(kernel, out_shape=(jax.ShapeDtypeStruct((2, 256, 512), BF1...  53.3 us
    unnamed x12, local copies, waits for them, and re-layouts  6.84 us

commit v1 on v0

--- a/solution.py
+++ b/solution.py
@@ -17,7 +17,7 @@
 F32 = jnp.float32
 BF16 = jnp.bfloat16
 
-P1, P3, P2, A2, DHI, DLO, EHI, ELO, BB = range(9)
+P1, P3, P2, A2, DHI, DLO, EHI, ELO, BB = range(-1, 8)
 
 
 def split16(table):
@@ -28,12 +28,13 @@
 
 def bf16_tables():
     out = np.zeros((9, 256, 256), ml_dtypes.bfloat16)
+    move = out[P1]
     for chan in range(64):
         for seq in range(2):
             for half in range(2):
                 row = (chan // 4) * 16 + seq * 8 + (chan % 4) * 2 + half
                 col = seq * 128 + half * 64 + chan
-                out[P1, row, col] = 1
+                move[row, col] = 1
                 out[P3, col, row] = 1
     for at in range(256):
         out[P2, (at % 16) * 16 + at // 16, at] = 1
@@ -50,7 +51,7 @@
     cos, sin = np.cos(turn), np.sin(turn)
     out[DHI], out[DLO] = split16(np.block([[cos, -sin], [sin, cos]]))
     out[EHI], out[ELO] = split16(np.block([[cos, sin], [-sin, cos]]))
-    return out
+    return move, out[:8]
 
 
 def f32_tables():
@@ -113,9 +114,9 @@
 
 
 def kernel(
-    og_hbm, gi_hbm, flt_hbm, tab_hbm, tw_hbm,
+    og_hbm, gi_hbm, flt_hbm, move_hbm, tab_hbm, tw_hbm,
     ig_out, fg_out,
-    og_in, gi_in, flt, tab, tw,
+    og_in, gi_in, flt, move, tab, tw,
     og_send, gi_send, ig_send, og_recv, gi_recv, ig_recv,
     rows, grad_spec, flt_spec, fg_part, fg_recv,
     in_sem, send_sem, recv_sem, fg_send_sem, fg_recv_sem,
@@ -126,7 +127,7 @@
     loads = [
         pltpu.make_async_copy(src, dst, in_sem.at[at])
         for at, (src, dst) in enumerate(
-            ((og_hbm, og_in), (tab_hbm, tab), (gi_hbm, gi_in), (flt_hbm, flt), (tw_hbm, tw))
+            ((move_hbm, move), (og_hbm, og_in), (gi_hbm, gi_in), (flt_hbm, flt), (tab_hbm, tab), (tw_hbm, tw))
         )
     ]
     for load in loads:
@@ -157,7 +158,7 @@
                 ],
                 0,
             )
-            target[pl.ds(pl.multiple_of(at * 256, 256), 256), :] = dot(tab[P1], block).astype(BF16)
+            target[pl.ds(pl.multiple_of(at * 256, 256), 256), :] = dot(move[...], block).astype(BF16)
             return 0
 
         lax.fori_loop(0, 4, group, 0)
@@ -194,6 +195,7 @@
     send_all(gi_send, gi_recv, 1)
     loads[3].wait()
     loads[4].wait()
+    loads[5].wait()
 
     def filter_spectrum(chan, _):
         taps = jnp.concatenate(
@@ -253,7 +255,18 @@
     wait_all(gi_recv, recv_sem, 1)
     to_rows(gi_recv)
 
-    def filter_grad(chan, _):
+    def part_copy(step):
+        return pltpu.make_async_remote_copy(
+            src_ref=fg_part.at[step],
+            dst_ref=fg_recv.at[step],
+            send_sem=fg_send_sem.at[step],
+            recv_sem=fg_recv_sem.at[step],
+            device_id={"rep": lax.rem(rep + 1 + step, REP)},
+            device_id_type=MESH,
+        )
+
+    def filter_grad(step, _):
+        chan = lax.rem(rep + 1 + step, REP)
         total_r = total_i = None
         for seq in range(2):
             at = chan + 4 * seq
@@ -263,26 +276,20 @@
             real, imag = sr * gr + si * gi, sr * gi - si * gr
             total_r = real if total_r is None else total_r + real
             total_i = imag if total_i is None else total_i + imag
-        fg_part[chan] = inverse(tab, tw, jnp.concatenate([total_r, total_i], 1))
-        return 0
-
-    lax.fori_loop(0, 4, filter_grad, 0)
-
-    for step in range(1, REP):
-        to = lax.rem(rep + step, REP)
-        pltpu.make_async_remote_copy(
-            src_ref=fg_part.at[to],
-            dst_ref=fg_recv.at[step - 1],
-            send_sem=fg_send_sem.at[step - 1],
-            recv_sem=fg_recv_sem.at[step - 1],
-            device_id={"rep": to},
-            device_id_type=MESH,
-        ).start()
-    total = fg_part[rep]
-    for step in range(1, REP):
-        slot = fg_recv.at[step - 1]
-        pltpu.make_async_copy(slot, slot, fg_recv_sem.at[step - 1]).wait()
-        total = total + fg_recv[step - 1]
+        fg_part[step] = inverse(tab, tw, jnp.concatenate([total_r, total_i], 1))
+
+        @pl.when(step < REP - 1)
+        def _():
+            part_copy(step).start()
+
+        return 0
+
+    lax.fori_loop(0, REP, filter_grad, 0)
+
+    total = fg_part[REP - 1]
+    for step in range(REP - 1):
+        part_copy(step).wait()
+        total = total + fg_recv[step]
     total = total * (1.0 / 512.0)
     for half in range(2):
         for high in range(2):
@@ -306,14 +313,12 @@
     wait_all(og_send, send_sem, 0)
     wait_all(gi_send, send_sem, 1)
     wait_all(ig_send, send_sem, 2)
-    for step in range(1, REP):
-        slot = fg_part.at[step - 1]
-        pltpu.make_async_copy(slot, slot, fg_send_sem.at[step - 1]).wait()
 
 
 def local(gated_input, out_grad, filter_taps):
+    move, tables = bf16_tables()
     taps = filter_taps.reshape(4, 256, 128).transpose(1, 0, 2).reshape(1024, 128)
-    any_spec = pl.BlockSpec(memory_space=pl.ANY)
+    hbm = pl.BlockSpec(memory_space=pltpu.HBM)
     vmem = pl.BlockSpec(memory_space=pltpu.VMEM)
     chunks = pltpu.VMEM((CTX * ROWS, 256), BF16)
     input_grad, filter_grad = pl.pallas_call(
@@ -322,13 +327,14 @@
             jax.ShapeDtypeStruct((2, 256, 512), BF16),
             jax.ShapeDtypeStruct((256, 128), F32),
         ),
-        in_specs=[any_spec] * 5,
+        in_specs=[hbm] * 6,
         out_specs=(vmem, vmem),
         scratch_shapes=[
             pltpu.VMEM((2, 256, 512), BF16),
             pltpu.VMEM((2, 256, 512), BF16),
             pltpu.VMEM((1024, 128), F32),
-            pltpu.VMEM((9, 256, 256), BF16),
+            pltpu.VMEM((256, 256), BF16),
+            pltpu.VMEM((8, 256, 256), BF16),
             pltpu.VMEM((128, 768), F32),
             chunks, chunks, chunks, chunks, chunks, chunks,
             chunks,
@@ -336,16 +342,24 @@
             pltpu.VMEM((4, 256, 256), F32),
             pltpu.VMEM((4, 128, 256), F32),
             pltpu.VMEM((3, 128, 256), F32),
-            pltpu.SemaphoreType.DMA((5,)),
+            pltpu.SemaphoreType.DMA((6,)),
             pltpu.SemaphoreType.DMA((3,)),
             pltpu.SemaphoreType.DMA((3,)),
             pltpu.SemaphoreType.DMA((3,)),
             pltpu.SemaphoreType.DMA((3,)),
         ],
         compiler_params=pltpu.CompilerParams(
-            collective_id=0, has_side_effects=True, vmem_limit_bytes=48 * 2**20
+            collective_id=0, has_side_effects=True, vmem_limit_bytes=40 * 2**20
         ),
-    )(out_grad, gated_input, taps, jnp.asarray(bf16_tables()), jnp.asarray(f32_tables()))
+    )(
+        *(
+            pltpu.with_memory_space_constraint(operand, pltpu.HBM)
+            for operand in (
+                out_grad, gated_input, taps,
+                jnp.asarray(move), jnp.asarray(tables), jnp.asarray(f32_tables()),
+            )
+        )
+    )
     return input_grad, filter_grad.reshape(1, 32768)
 
 

time: 61.4 us -> 53.6 us (0.87)
  local copies, waits for them, and re-layouts: 6.84 us -> 1.45 us
  Pallas kernels: 53.3 us -> 51.3 us
    unnamed x12 -> x2, local copies, waits for them, and re-layouts: 6.84 us -> 1.45 us
    pallas_call x1, Pallas kernels: 53.3 us -> 51.3 us  [local(): pl.pallas_call(kernel, out_shape=(jax.ShapeDtypeStruct((2, 256, 512), BF1...]
where the time goes in v1:
time: 53.6 us; the launch traced here: 53.4 us
  Pallas kernels  51.3 us (96%)
  local copies, waits for them, and re-layouts  1.45 us (3%)
  between operations  0.64 us (1%)
    pallas_call x1, Pallas kernels, local(): pl.pallas_call(kernel, out_shape=(jax.ShapeDtypeStruct((2, 256, 512), BF1...  51.3 us
    unnamed x2, local copies, waits for them, and re-layouts  1.45 us

profile of v1, /device:TPU:1, one launch (start us, length us, event | category | flops | bytes accessed | tf_op | source)
XLA Modules:
  0.0 53.4 jit_solution(14955998150522403056)
XLA Ops:
  0.6 51.3 %shard_map.77 = (bf16[2,256,512]{2,1,0:T(8,128)(2,1)S(1)}, f32[256,128]{1,0:T(8,128)S(1)}) custom-call(bf16[2,256,512]{2,1,0:T(8,128)(2,1)} %og_hbm.1, bf16[2,256,512]{2,1,0:T(8,128)(2,1)} %gi_hbm.1, f32[1024,128]{1,0:T(8,128)} %bitcast.7, bf16[256,256]{1,0:T(8,128)(2,1)} %constant.6.clone.move_hbm, bf16[8,256,256]{2,1,0:T(8,128)(2,1)} %constant.7.clone.tab_hbm, ...), custom_call_target="tpu_custom_call" | custom-call | tf_op jit(solution)/shard_map/pallas_call | solution.py:324
  52.0 0.8 %copy.11 = bf16[2,256,512]{2,1,0:T(8,128)(2,1)} copy(bf16[2,256,512]{2,1,0:T(8,128)(2,1)S(1)} %get-tuple-element.8) | data formatting | bytes 1048576
  52.8 0.7 %copy.12 = f32[1,32768]{1,0:T(1,128)} copy(f32[1,32768]{1,0:T(1,128)S(1)} %bitcast.6) | data formatting | bytes 262144

commit v2 on v1

--- a/solution.py
+++ b/solution.py
@@ -77,40 +77,55 @@
     return ar * br - ai * bi, ar * bi + ai * br
 
 
-def forward_tail(tab, tw, step):
-    t0r, t1r = tw[:, 0:128], tw[:, 128:256]
-    t0i, t1i = tw[:, 256:384], tw[:, 384:512]
-    wr, wi = tw[:, 512:640], tw[:, 640:768]
-    z0r, z0i = cmul(step[:128, :128], step[128:, :128], t0r, t0i)
-    z1r, z1i = cmul(step[:128, 128:], step[128:, 128:], t1r, t1i)
-    odd_r, odd_i = cmul(z0r - z1r, z0i - z1i, wr, wi)
-    both = jnp.concatenate(
-        [
-            jnp.concatenate([z0r + z1r, z0i + z1i], 1),
-            jnp.concatenate([odd_r, odd_i], 1),
-        ],
-        0,
+def twiddles(tw):
+    return (
+        (tw[:, 0:128], tw[:, 256:384]),
+        (tw[:, 128:256], tw[:, 384:512]),
+        (tw[:, 512:640], tw[:, 640:768]),
     )
-    high, low = halves(both)
-    return dot(high, tab[DHI]) + dot(low, tab[DHI]) + dot(high, tab[DLO])
-
-
-def inverse(tab, tw, spec):
-    high, low = halves(spec)
-    back = dot(high, tab[EHI]) + dot(low, tab[EHI]) + dot(high, tab[ELO])
-    t0r, t1r = tw[:, 0:128], tw[:, 128:256]
-    t0i, t1i = tw[:, 256:384], tw[:, 384:512]
-    wr, wi = tw[:, 512:640], tw[:, 640:768]
-    er, ei = back[:128, :128], back[:128, 128:]
-    dr, di = cmul(back[128:, :128], back[128:, 128:], wr, -wi)
-    a0r, a0i = cmul(er + dr, ei + di, t0r, -t0i)
-    a1r, a1i = cmul(er - dr, ei - di, t1r, -t1i)
-    stack = jnp.concatenate(
-        [jnp.concatenate([a0r, a1r], 1), jnp.concatenate([a0i, a1i], 1)], 0
-    )
-    high, low = halves(stack)
+
+
+def transform(rows, table_high, table_low):
+    count = rows.shape[0]
+    high, low = halves(rows)
+    wide = dot(jnp.concatenate([high, low], 0), table_high)
+    return wide[:count] + wide[count:] + dot(high, table_low)
+
+
+def forward(tab, tw, step, count):
+    (t0r, t0i), (t1r, t1i), (wr, wi) = twiddles(tw)
+    rows = []
+    for at in range(count):
+        lanes = 256 * at
+        z0r, z0i = cmul(step[:128, lanes : lanes + 128], step[128:, lanes : lanes + 128], t0r, t0i)
+        z1r, z1i = cmul(step[:128, lanes + 128 : lanes + 256], step[128:, lanes + 128 : lanes + 256], t1r, t1i)
+        odd_r, odd_i = cmul(z0r - z1r, z0i - z1i, wr, wi)
+        rows.append(jnp.concatenate([z0r + z1r, z0i + z1i], 1))
+        rows.append(jnp.concatenate([odd_r, odd_i], 1))
+    spec = transform(jnp.concatenate(rows, 0), tab[DHI], tab[DLO])
+    return [spec[256 * at : 256 * at + 256] for at in range(count)]
+
+
+def inverse(tab, tw, specs):
+    (t0r, t0i), (t1r, t1i), (wr, wi) = twiddles(tw)
+    back = transform(jnp.concatenate(specs, 0), tab[EHI], tab[ELO])
+    columns = []
+    for at in range(len(specs)):
+        even = back[256 * at : 256 * at + 128]
+        odd = back[256 * at + 128 : 256 * at + 256]
+        er, ei = even[:, :128], even[:, 128:]
+        dr, di = cmul(odd[:, :128], odd[:, 128:], wr, -wi)
+        a0r, a0i = cmul(er + dr, ei + di, t0r, -t0i)
+        a1r, a1i = cmul(er - dr, ei - di, t1r, -t1i)
+        columns.append(
+            jnp.concatenate(
+                [jnp.concatenate([a0r, a1r], 1), jnp.concatenate([a0i, a1i], 1)], 0
+            )
+        )
+    high, low = halves(jnp.concatenate(columns, 1))
     wide = dot(tab[BB], high)
-    return wide[:128] + wide[128:] + dot(tab[BB, :128, :], low)
+    out = wide[:128] + wide[128:] + dot(tab[BB, :128, :], low)
+    return [out[:, 256 * at : 256 * at + 256] for at in range(len(specs))]
 
 
 def kernel(
@@ -142,10 +157,11 @@
         return 0
 
     lax.fori_loop(1, CTX, greet, 0)
-    for step in range(1, REP):
-        pl.semaphore_signal(
-            barrier, inc=1, device_id={"rep": lax.rem(rep + step, REP)}, device_id_type=MESH
-        )
+    core, high_y = lax.rem(rep, 2), rep // 2
+    near = 2 * high_y + 1 - core
+    far = 2 * (1 - high_y) + core
+    for peer in (near, far):
+        pl.semaphore_signal(barrier, inc=1, device_id={"rep": peer}, device_id_type=MESH)
 
     def arrange(source, target):
         def group(at, _):
@@ -161,13 +177,14 @@
             target[pl.ds(pl.multiple_of(at * 256, 256), 256), :] = dot(move[...], block).astype(BF16)
             return 0
 
-        lax.fori_loop(0, 4, group, 0)
+        lax.fori_loop(0, 4, group, 0, unroll=True)
 
     mine = pl.ds(pl.multiple_of(me * ROWS, ROWS), ROWS)
 
     def send_all(source, target, which):
         def send(step, _):
-            to = lax.rem(me + step, CTX)
+            away = jnp.where(step % 2 == 1, (step + 1) // 2, CTX - step // 2)
+            to = lax.rem(me + away, CTX)
             pltpu.make_async_remote_copy(
                 src_ref=source.at[pl.ds(pl.multiple_of(to * ROWS, ROWS), ROWS), :],
                 dst_ref=target.at[mine, :],
@@ -179,6 +196,8 @@
             return 0
 
         lax.fori_loop(1, CTX, send, 0)
+
+    def keep_own(source, target):
         target[mine, :] = source[mine, :]
 
     def wait_all(buffer, sems, which):
@@ -188,11 +207,13 @@
     loads[0].wait()
     loads[1].wait()
     arrange(og_in, og_send)
-    pl.semaphore_wait(barrier, CTX - 1 + REP - 1)
+    pl.semaphore_wait(barrier, CTX - 1 + 2)
     send_all(og_send, og_recv, 0)
+    keep_own(og_send, og_recv)
     loads[2].wait()
     arrange(gi_in, gi_send)
     send_all(gi_send, gi_recv, 1)
+    keep_own(gi_send, gi_recv)
     loads[3].wait()
     loads[4].wait()
     loads[5].wait()
@@ -209,7 +230,7 @@
         )
         high, low = halves(taps)
         step = dot(tab[A2], jnp.concatenate([high, high], 0)) + dot(tab[A2, :, :128], low)
-        flt_spec[chan] = forward_tail(tab, tw, step)
+        (flt_spec[chan],) = forward(tab, tw, step, 1)
         return 0
 
     lax.fori_loop(0, 4, filter_spectrum, 0)
@@ -222,25 +243,34 @@
                 rows[pl.ds(pl.multiple_of(row * 64 + at * 16, 16), 16), :] = turned[row * 16 : row * 16 + 16]
             return 0
 
-        lax.fori_loop(0, 4, group, 0)
-
-    def spectrum(at):
-        block = rows[pl.ds(pl.multiple_of(at * 128, 128), 128), :]
-        return forward_tail(tab, tw, dot(tab[A2], jnp.concatenate([block, block], 0)))
+        lax.fori_loop(0, 4, group, 0, unroll=True)
+
+    def spectra(ats):
+        blocks = jnp.concatenate(
+            [rows[pl.ds(pl.multiple_of(at * 128, 128), 128), :] for at in ats], 1
+        )
+        step = dot(tab[A2], jnp.concatenate([blocks, blocks], 0))
+        return forward(tab, tw, step, len(ats))
 
     wait_all(og_recv, recv_sem, 0)
     to_rows(og_recv)
 
-    def input_grad(at, _):
-        spec = spectrum(at)
-        grad_spec[at] = spec
-        taps = flt_spec[lax.rem(at, 4)]
-        sr, si, fr, fi = spec[:, :128], spec[:, 128:], taps[:, :128], taps[:, 128:]
-        corr = jnp.concatenate([fr * sr + fi * si, fr * si - fi * sr], 1)
-        rows[pl.ds(pl.multiple_of(at * 128, 128), 128), :] = inverse(tab, tw, corr).astype(BF16)
-        return 0
-
-    lax.fori_loop(0, 8, input_grad, 0)
+    def input_grad(chan, _):
+        ats = (chan, chan + 4)
+        taps = flt_spec[chan]
+        fr, fi = taps[:, :128], taps[:, 128:]
+        specs = spectra(ats)
+        corrs = []
+        for spec in specs:
+            sr, si = spec[:, :128], spec[:, 128:]
+            corrs.append(jnp.concatenate([fr * sr + fi * si, fr * si - fi * sr], 1))
+        grads = inverse(tab, tw, corrs)
+        for at, spec, grad in zip(ats, specs, grads, strict=True):
+            grad_spec[at] = spec
+            rows[pl.ds(pl.multiple_of(at * 128, 128), 128), :] = grad.astype(BF16)
+        return 0
+
+    lax.fori_loop(0, 4, input_grad, 0)
 
     def from_rows(at, _):
         block = jnp.concatenate(
@@ -249,47 +279,56 @@
         ig_send[pl.ds(pl.multiple_of(at * 256, 256), 256), :] = dot(tab[P2], block).astype(BF16)
         return 0
 
-    lax.fori_loop(0, 4, from_rows, 0)
+    lax.fori_loop(0, 4, from_rows, 0, unroll=True)
     send_all(ig_send, ig_recv, 2)
+    keep_own(ig_send, ig_recv)
 
     wait_all(gi_recv, recv_sem, 1)
     to_rows(gi_recv)
 
-    def part_copy(step):
+    def part_copy(slot, peer):
         return pltpu.make_async_remote_copy(
-            src_ref=fg_part.at[step],
-            dst_ref=fg_recv.at[step],
-            send_sem=fg_send_sem.at[step],
-            recv_sem=fg_recv_sem.at[step],
-            device_id={"rep": lax.rem(rep + 1 + step, REP)},
+            src_ref=fg_part.at[slot],
+            dst_ref=fg_recv.at[slot],
+            send_sem=fg_send_sem.at[slot],
+            recv_sem=fg_recv_sem.at[slot],
+            device_id={"rep": peer},
             device_id_type=MESH,
         )
 
-    def filter_grad(step, _):
-        chan = lax.rem(rep + 1 + step, REP)
+    def filter_grad(chan):
+        ats = (chan, chan + 4)
         total_r = total_i = None
-        for seq in range(2):
-            at = chan + 4 * seq
-            spec = spectrum(at)
+        for at, spec in zip(ats, spectra(ats), strict=True):
             grad = grad_spec[at]
             sr, si, gr, gi = spec[:, :128], spec[:, 128:], grad[:, :128], grad[:, 128:]
             real, imag = sr * gr + si * gi, sr * gi - si * gr
             total_r = real if total_r is None else total_r + real
             total_i = imag if total_i is None else total_i + imag
-        fg_part[step] = inverse(tab, tw, jnp.concatenate([total_r, total_i], 1))
-
-        @pl.when(step < REP - 1)
+        (part,) = inverse(tab, tw, [jnp.concatenate([total_r, total_i], 1)])
+        return part
+
+    def filter_grads(step, _):
+        chan = jnp.where(step // 2 == 0, 2 * (1 - high_y), 2 * high_y)
+        chan = chan + jnp.where(lax.rem(step, 2) == 0, 1 - core, core)
+        fg_part[step] = filter_grad(chan)
+
+        @pl.when(lax.rem(step, 2) == 0)
         def _():
-            part_copy(step).start()
-
-        return 0
-
-    lax.fori_loop(0, REP, filter_grad, 0)
-
-    total = fg_part[REP - 1]
-    for step in range(REP - 1):
-        part_copy(step).wait()
-        total = total + fg_recv[step]
+            part_copy(step, near).start()
+
+        @pl.when(step == 1)
+        def _():
+            part_copy(0, near).wait()
+            fg_part[1] += fg_recv[0]
+            part_copy(1, far).start()
+
+        return 0
+
+    lax.fori_loop(0, REP, filter_grads, 0)
+    part_copy(1, far).wait()
+    part_copy(2, near).wait()
+    total = fg_part[3] + fg_recv[2] + fg_recv[1]
     total = total * (1.0 / 512.0)
     for half in range(2):
         for high in range(2):
@@ -309,7 +348,7 @@
                 ig_out[seq, chans, half * 256 : half * 256 + 256] = turned[start : start + 64]
         return 0
 
-    lax.fori_loop(0, 4, finish, 0)
+    lax.fori_loop(0, 4, finish, 0, unroll=True)
     wait_all(og_send, send_sem, 0)
     wait_all(gi_send, send_sem, 1)
     wait_all(ig_send, send_sem, 2)

time: 53.6 us -> 51.2 us (0.955)
  Pallas kernels: 51.3 us -> 49.1 us
    pallas_call x1, Pallas kernels: 51.3 us -> 49.1 us  [local(): pl.pallas_call(kernel, out_shape=(jax.ShapeDtypeStruct((2, 256, 512), BF1...]
where the time goes in v2:
time: 51.2 us
  Pallas kernels  49.1 us (96%)
  local copies, waits for them, and re-layouts  1.45 us (3%)
  between operations  0.64 us (1%)
    pallas_call x1, Pallas kernels, local(): pl.pallas_call(kernel, out_shape=(jax.ShapeDtypeStruct((2, 256, 512), BF1...  49.1 us
    unnamed x2, local copies, waits for them, and re-layouts  1.45 us

profile of v2, /device:TPU:1, one launch (start us, length us, event | category | flops | bytes accessed | tf_op | source)
XLA Modules:
  0.0 51.2 jit_solution(5609110115682049359)
XLA Ops:
  0.6 49.1 %shard_map.77 = (bf16[2,256,512]{2,1,0:T(8,128)(2,1)S(1)}, f32[256,128]{1,0:T(8,128)S(1)}) custom-call(bf16[2,256,512]{2,1,0:T(8,128)(2,1)} %og_hbm.1, bf16[2,256,512]{2,1,0:T(8,128)(2,1)} %gi_hbm.1, f32[1024,128]{1,0:T(8,128)} %bitcast.7, bf16[256,256]{1,0:T(8,128)(2,1)} %constant.6.clone.move_hbm, bf16[8,256,256]{2,1,0:T(8,128)(2,1)} %constant.7.clone.tab_hbm, ...), custom_call_target="tpu_custom_call" | custom-call | tf_op jit(solution)/shard_map/pallas_call | solution.py:363
  49.7 0.8 %copy.11 = bf16[2,256,512]{2,1,0:T(8,128)(2,1)} copy(bf16[2,256,512]{2,1,0:T(8,128)(2,1)S(1)} %get-tuple-element.8) | data formatting | bytes 1048576
  50.5 0.7 %copy.12 = f32[1,32768]{1,0:T(1,128)} copy(f32[1,32768]{1,0:T(1,128)S(1)} %bitcast.6) | data formatting | bytes 262144

commit v3 on v2

--- a/solution.py
+++ b/solution.py
@@ -17,7 +17,7 @@
 F32 = jnp.float32
 BF16 = jnp.bfloat16
 
-P1, P3, P2, A2, DHI, DLO, EHI, ELO, BB = range(-1, 8)
+P2, A2, DHI, DLO, EHI, ELO, BB = range(7)
 
 
 def split16(table):
@@ -27,15 +27,14 @@
 
 
 def bf16_tables():
-    out = np.zeros((9, 256, 256), ml_dtypes.bfloat16)
-    move = out[P1]
+    out = np.zeros((7, 256, 256), ml_dtypes.bfloat16)
+    move = np.zeros((256, 256), ml_dtypes.bfloat16)
     for chan in range(64):
         for seq in range(2):
             for half in range(2):
                 row = (chan // 4) * 16 + seq * 8 + (chan % 4) * 2 + half
                 col = seq * 128 + half * 64 + chan
                 move[row, col] = 1
-                out[P3, col, row] = 1
     for at in range(256):
         out[P2, (at % 16) * 16 + at // 16, at] = 1
     place = np.arange(128)
@@ -51,7 +50,16 @@
     cos, sin = np.cos(turn), np.sin(turn)
     out[DHI], out[DLO] = split16(np.block([[cos, -sin], [sin, cos]]))
     out[EHI], out[ELO] = split16(np.block([[cos, sin], [-sin, cos]]))
-    return move, out[:8]
+    return move, out
+
+
+def pair_moves():
+    out = np.zeros((2, 256, 512), ml_dtypes.bfloat16)
+    for pair in range(2):
+        for row in range(256):
+            dest, seq, chan, half, high = row // 16, row // 8 % 2, row // 4 % 2, row // 2 % 2, row % 2
+            out[pair, row, high * 256 + seq * 128 + half * 64 + dest * 4 + 2 * pair + chan] = 1
+    return out
 
 
 def f32_tables():
@@ -129,10 +137,10 @@
 
 
 def kernel(
-    og_hbm, gi_hbm, flt_hbm, move_hbm, tab_hbm, tw_hbm,
-    ig_out, fg_out,
-    og_in, gi_in, flt, move, tab, tw,
-    og_send, gi_send, ig_send, og_recv, gi_recv, ig_recv,
+    og_hbm, gi_hbm, flt_hbm, move_hbm, pair_hbm, tab_hbm, tw_hbm,
+    ig_recv, fg_total,
+    og_in, gi_in, flt, move, pair_move, tab, tw,
+    og_send, gi_send0, gi_send1, ig_send, og_recv, gi_recv0, gi_recv1,
     rows, grad_spec, flt_spec, fg_part, fg_recv,
     in_sem, send_sem, recv_sem, fg_send_sem, fg_recv_sem,
 ):
@@ -142,7 +150,7 @@
     loads = [
         pltpu.make_async_copy(src, dst, in_sem.at[at])
         for at, (src, dst) in enumerate(
-            ((move_hbm, move), (og_hbm, og_in), (gi_hbm, gi_in), (flt_hbm, flt), (tab_hbm, tab), (tw_hbm, tw))
+            ((move_hbm, move), (og_hbm, og_in), (gi_hbm, gi_in), (pair_hbm, pair_move), (flt_hbm, flt), (tab_hbm, tab), (tw_hbm, tw))
         )
     ]
     for load in loads:
@@ -156,28 +164,22 @@
         )
         return 0
 
-    lax.fori_loop(1, CTX, greet, 0)
+    lax.fori_loop(1, CTX, greet, 0, unroll=7)
     core, high_y = lax.rem(rep, 2), rep // 2
     near = 2 * high_y + 1 - core
     far = 2 * (1 - high_y) + core
     for peer in (near, far):
         pl.semaphore_signal(barrier, inc=1, device_id={"rep": peer}, device_id_type=MESH)
 
-    def arrange(source, target):
-        def group(at, _):
-            chans = pl.ds(pl.multiple_of(at * 64, 64), 64)
-            block = jnp.concatenate(
-                [
-                    source[seq, chans, half * 256 : half * 256 + 256]
-                    for seq in range(2)
-                    for half in range(2)
-                ],
-                0,
-            )
-            target[pl.ds(pl.multiple_of(at * 256, 256), 256), :] = dot(move[...], block).astype(BF16)
-            return 0
-
-        lax.fori_loop(0, 4, group, 0, unroll=True)
+    def gather(source, at):
+        return jnp.concatenate(
+            [
+                source[seq, 64 * at : 64 * at + 64, half * 256 : half * 256 + 256]
+                for seq in range(2)
+                for half in range(2)
+            ],
+            0,
+        )
 
     mine = pl.ds(pl.multiple_of(me * ROWS, ROWS), ROWS)
 
@@ -195,7 +197,7 @@
             ).start()
             return 0
 
-        lax.fori_loop(1, CTX, send, 0)
+        lax.fori_loop(1, CTX, send, 0, unroll=7)
 
     def keep_own(source, target):
         target[mine, :] = source[mine, :]
@@ -206,17 +208,24 @@
 
     loads[0].wait()
     loads[1].wait()
-    arrange(og_in, og_send)
+    for at in range(4):
+        og_send[256 * at : 256 * at + 256, :] = dot(move[...], gather(og_in, at)).astype(BF16)
     pl.semaphore_wait(barrier, CTX - 1 + 2)
     send_all(og_send, og_recv, 0)
     keep_own(og_send, og_recv)
     loads[2].wait()
-    arrange(gi_in, gi_send)
-    send_all(gi_send, gi_recv, 1)
-    keep_own(gi_send, gi_recv)
     loads[3].wait()
+    pairs = ((gi_send0, gi_recv0, 1 - high_y), (gi_send1, gi_recv1, high_y))
+    for which, (source, target, pair) in enumerate(pairs):
+        for at in range(4):
+            block = gather(gi_in, at)
+            block = jnp.concatenate([block[:, :128], block[:, 128:]], 0)
+            source[256 * at : 256 * at + 256, :] = dot(pair_move[pair], block).astype(BF16)
+        send_all(source, target, 1 + which)
+        keep_own(source, target)
     loads[4].wait()
     loads[5].wait()
+    loads[6].wait()
 
     def filter_spectrum(chan, _):
         taps = jnp.concatenate(
@@ -236,14 +245,21 @@
     lax.fori_loop(0, 4, filter_spectrum, 0)
 
     def to_rows(buffer):
-        def group(at, _):
-            block = buffer[pl.ds(pl.multiple_of(at * 256, 256), 256), :]
-            turned = dot(tab[P2], block).astype(BF16)
+        for at in range(4):
+            turned = dot(tab[P2], buffer[256 * at : 256 * at + 256, :]).astype(BF16)
             for row in range(16):
-                rows[pl.ds(pl.multiple_of(row * 64 + at * 16, 16), 16), :] = turned[row * 16 : row * 16 + 16]
-            return 0
-
-        lax.fori_loop(0, 4, group, 0, unroll=True)
+                start = row * 64 + at * 16
+                rows[start : start + 16, :] = turned[row * 16 : row * 16 + 16]
+
+    def pair_to_rows(buffer, pair):
+        for at in range(4):
+            turned = dot(tab[P2], buffer[256 * at : 256 * at + 256, :]).astype(BF16)
+            for row in range(16):
+                seq, chan, half, high = row // 8, row // 4 % 2, row // 2 % 2, row % 2
+                start = pair * 256 + seq * 512 + chan * 128 + half * 64 + at * 16
+                rows[pl.ds(pl.multiple_of(start, 16), 16), 128 * high : 128 * high + 128] = turned[
+                    row * 16 : row * 16 + 16
+                ]
 
     def spectra(ats):
         blocks = jnp.concatenate(
@@ -280,11 +296,8 @@
         return 0
 
     lax.fori_loop(0, 4, from_rows, 0, unroll=True)
-    send_all(ig_send, ig_recv, 2)
+    send_all(ig_send, ig_recv, 3)
     keep_own(ig_send, ig_recv)
-
-    wait_all(gi_recv, recv_sem, 1)
-    to_rows(gi_recv)
 
     def part_copy(slot, peer):
         return pltpu.make_async_remote_copy(
@@ -308,50 +321,63 @@
         (part,) = inverse(tab, tw, [jnp.concatenate([total_r, total_i], 1)])
         return part
 
-    def filter_grads(step, _):
-        chan = jnp.where(step // 2 == 0, 2 * (1 - high_y), 2 * high_y)
-        chan = chan + jnp.where(lax.rem(step, 2) == 0, 1 - core, core)
-        fg_part[step] = filter_grad(chan)
-
-        @pl.when(lax.rem(step, 2) == 0)
-        def _():
-            part_copy(step, near).start()
-
-        @pl.when(step == 1)
-        def _():
+    for which, (_, target, pair) in enumerate(pairs):
+        wait_all(target, recv_sem, 1 + which)
+        pair_to_rows(target, pair)
+
+        def filter_grads(step, _):
+            chan = 2 * pair + jnp.where(step == 0, 1 - core, core)
+            fg_part[2 * which + step] = filter_grad(chan)
+
+            @pl.when(step == 0)
+            def _():
+                part_copy(2 * which, near).start()
+
+            return 0
+
+        lax.fori_loop(0, 2, filter_grads, 0)
+        if which == 0:
             part_copy(0, near).wait()
             fg_part[1] += fg_recv[0]
             part_copy(1, far).start()
-
-        return 0
-
-    lax.fori_loop(0, REP, filter_grads, 0)
     part_copy(1, far).wait()
     part_copy(2, near).wait()
     total = fg_part[3] + fg_recv[2] + fg_recv[1]
-    total = total * (1.0 / 512.0)
+    fg_total[...] = total
+    wait_all(ig_recv, recv_sem, 3)
+    wait_all(og_send, send_sem, 0)
+    wait_all(gi_send0, send_sem, 1)
+    wait_all(gi_send1, send_sem, 2)
+    wait_all(ig_send, send_sem, 3)
+
+
+def finish(chunk_rows, total, ig_hbm, fg_hbm, ig_out, fg_out, sem):
+    scaled = total[...] * (1.0 / 512.0)
     for half in range(2):
         for high in range(2):
-            fg_out[pl.ds(2 * half + high, 64, stride=4), :] = total[
+            fg_out[pl.ds(2 * half + high, 64, stride=4), :] = scaled[
                 half * 64 : half * 64 + 64, high * 128 : high * 128 + 128
             ]
-
-    wait_all(ig_recv, recv_sem, 2)
-
-    def finish(at, _):
-        block = ig_recv[pl.ds(pl.multiple_of(at * 256, 256), 256), :]
-        turned = dot(tab[P3], block).astype(BF16)
-        chans = pl.ds(pl.multiple_of(at * 64, 64), 64)
+    copies = [pltpu.make_async_copy(fg_out, fg_hbm, sem.at[4])]
+    copies[0].start()
+    row = lax.broadcasted_iota(jnp.int32, (256, 256), 0)
+    col = lax.broadcasted_iota(jnp.int32, (256, 256), 1)
+    chan = row % 64
+    source = chan // 4 * 16 + row // 128 * 8 + chan % 4 * 2 + row // 64 % 2
+    move = jnp.where(source == col, 1.0, 0.0).astype(BF16)
+    for at in range(4):
+        turned = dot(move, chunk_rows[256 * at : 256 * at + 256, :]).astype(BF16)
+        chans = pl.ds(64 * at, 64)
         for seq in range(2):
             for half in range(2):
                 start = seq * 128 + half * 64
                 ig_out[seq, chans, half * 256 : half * 256 + 256] = turned[start : start + 64]
-        return 0
-
-    lax.fori_loop(0, 4, finish, 0, unroll=True)
-    wait_all(og_send, send_sem, 0)
-    wait_all(gi_send, send_sem, 1)
-    wait_all(ig_send, send_sem, 2)
+        copies.append(
+            pltpu.make_async_copy(ig_out.at[:, chans, :], ig_hbm.at[:, chans, :], sem.at[at])
+        )
+        copies[-1].start()
+    for copy in copies:
+        copy.wait()
 
 
 def local(gated_input, out_grad, filter_taps):
@@ -360,30 +386,32 @@
     hbm = pl.BlockSpec(memory_space=pltpu.HBM)
     vmem = pl.BlockSpec(memory_space=pltpu.VMEM)
     chunks = pltpu.VMEM((CTX * ROWS, 256), BF16)
-    input_grad, filter_grad = pl.pallas_call(
+    pair_chunks = pltpu.VMEM((CTX * ROWS, 128), BF16)
+    chunk_rows, total = pl.pallas_call(
         kernel,
         out_shape=(
-            jax.ShapeDtypeStruct((2, 256, 512), BF16),
-            jax.ShapeDtypeStruct((256, 128), F32),
+            jax.ShapeDtypeStruct((CTX * ROWS, 256), BF16),
+            jax.ShapeDtypeStruct((128, 256), F32),
         ),
-        in_specs=[hbm] * 6,
+        in_specs=[hbm] * 7,
         out_specs=(vmem, vmem),
         scratch_shapes=[
             pltpu.VMEM((2, 256, 512), BF16),
             pltpu.VMEM((2, 256, 512), BF16),
             pltpu.VMEM((1024, 128), F32),
             pltpu.VMEM((256, 256), BF16),
-            pltpu.VMEM((8, 256, 256), BF16),
+            pltpu.VMEM((2, 256, 512), BF16),
+            pltpu.VMEM((7, 256, 256), BF16),
             pltpu.VMEM((128, 768), F32),
-            chunks, chunks, chunks, chunks, chunks, chunks,
+            chunks, pair_chunks, pair_chunks, chunks, chunks, pair_chunks, pair_chunks,
             chunks,
             pltpu.VMEM((8, 256, 256), F32),
             pltpu.VMEM((4, 256, 256), F32),
             pltpu.VMEM((4, 128, 256), F32),
             pltpu.VMEM((3, 128, 256), F32),
-            pltpu.SemaphoreType.DMA((6,)),
-            pltpu.SemaphoreType.DMA((3,)),
-            pltpu.SemaphoreType.DMA((3,)),
+            pltpu.SemaphoreType.DMA((7,)),
+            pltpu.SemaphoreType.DMA((4,)),
+            pltpu.SemaphoreType.DMA((4,)),
             pltpu.SemaphoreType.DMA((3,)),
             pltpu.SemaphoreType.DMA((3,)),
         ],
@@ -395,10 +423,25 @@
             pltpu.with_memory_space_constraint(operand, pltpu.HBM)
             for operand in (
                 out_grad, gated_input, taps,
-                jnp.asarray(move), jnp.asarray(tables), jnp.asarray(f32_tables()),
+                jnp.asarray(move), jnp.asarray(pair_moves()), jnp.asarray(tables), jnp.asarray(f32_tables()),
             )
         )
     )
+    input_grad, filter_grad = pl.pallas_call(
+        finish,
+        out_shape=(
+            jax.ShapeDtypeStruct((2, 256, 512), BF16),
+            jax.ShapeDtypeStruct((256, 128), F32),
+        ),
+        in_specs=[vmem, vmem],
+        out_specs=(pl.BlockSpec(memory_space=pl.ANY),) * 2,
+        scratch_shapes=[
+            pltpu.VMEM((2, 256, 512), BF16),
+            pltpu.VMEM((256, 128), F32),
+            pltpu.SemaphoreType.DMA((5,)),
+        ],
+        compiler_params=pltpu.CompilerParams(vmem_limit_bytes=16 * 2**20),
+    )(chunk_rows, total)
     return input_grad, filter_grad.reshape(1, 32768)
 
 

time: 51.2 us -> 49.2 us (0.961)
  the two profiles are of different devices: /device:TPU:1 before, /device:TPU:32 now
where the time goes in v3:
time: 49.2 us
  Pallas kernels  48.5 us (99%)
  between operations  0.64 us (1%)
    pallas_call x1, Pallas kernels, local(): pl.pallas_call(kernel, out_shape=(jax.ShapeDtypeStruct((CTX * ROWS, 256),...  47.4 us
    pallas_call x1, Pallas kernels, local(): pl.pallas_call(finish, out_shape=(jax.ShapeDtypeStruct((2, 256, 512), BF1...  1.07 us

profile of v3, /device:TPU:32, one launch (start us, length us, event | category | flops | bytes accessed | tf_op | source)
XLA Modules:
  0.0 49.2 jit_solution(4452088571824948730)
XLA Ops:
  0.6 47.4 %shard_map.86 = (bf16[1024,256]{1,0:T(8,128)(2,1)S(1)}, f32[128,256]{1,0:T(8,128)S(1)}) custom-call(bf16[2,256,512]{2,1,0:T(8,128)(2,1)} %og_hbm.1, bf16[2,256,512]{2,1,0:T(8,128)(2,1)} %gi_hbm.1, f32[1024,128]{1,0:T(8,128)} %bitcast.6, bf16[256,256]{1,0:T(8,128)(2,1)} %constant.8.clone.move_hbm, bf16[2,256,512]{2,1,0:T(8,128)(2,1)} %constant.9.clone.pair_hbm, ...), custom_call_target="tpu_custom_call" | custom-call | tf_op jit(solution)/shard_map/pallas_call | solution.py:390
  48.1 1.1 %shard_map.87 = (bf16[2,256,512]{2,1,0:T(8,128)(2,1)}, f32[256,128]{1,0:T(8,128)}) custom-call(bf16[1024,256]{1,0:T(8,128)(2,1)S(1)} %get-tuple-element.6.chunk_rows, f32[128,256]{1,0:T(8,128)S(1)} %get-tuple-element.7.total), custom_call_target="tpu_custom_call" | custom-call | tf_op jit(solution)/shard_map/pallas_call | solution.py:430

commit v4 on v3

--- a/solution.py
+++ b/solution.py
@@ -159,12 +159,13 @@
     barrier = pltpu.get_barrier_semaphore()
 
     def greet(step, _):
+        away = jnp.where(step % 2 == 1, 32 - step // 2, 32 + step // 2)
         pl.semaphore_signal(
-            barrier, inc=1, device_id={"ctx": lax.rem(me + step, CTX)}, device_id_type=MESH
+            barrier, inc=1, device_id={"ctx": lax.rem(me + away, CTX)}, device_id_type=MESH
         )
         return 0
 
-    lax.fori_loop(1, CTX, greet, 0, unroll=7)
+    lax.fori_loop(1, CTX, greet, 0, unroll=21)
     core, high_y = lax.rem(rep, 2), rep // 2
     near = 2 * high_y + 1 - core
     far = 2 * (1 - high_y) + core

time: 49.2 us -> 48.5 us (0.986)
  the two profiles are of different devices: /device:TPU:32 before, /device:TPU:1 now
where the time goes in v4:
time: 48.5 us; the launch traced here: 48.2 us
  Pallas kernels  47.6 us (98%)
  between operations  0.64 us (1%)
    pallas_call x1, Pallas kernels, local(): pl.pallas_call(kernel, out_shape=(jax.ShapeDtypeStruct((CTX * ROWS, 256),...  46.5 us
    pallas_call x1, Pallas kernels, local(): pl.pallas_call(finish, out_shape=(jax.ShapeDtypeStruct((2, 256, 512), BF1...  1.06 us

profile of v4, /device:TPU:1, one launch (start us, length us, event | category | flops | bytes accessed | tf_op | source)
XLA Modules:
  0.0 48.2 jit_solution(16145608874850183087)
XLA Ops:
  0.6 46.5 %shard_map.86 = (bf16[1024,256]{1,0:T(8,128)(2,1)S(1)}, f32[128,256]{1,0:T(8,128)S(1)}) custom-call(bf16[2,256,512]{2,1,0:T(8,128)(2,1)} %og_hbm.1, bf16[2,256,512]{2,1,0:T(8,128)(2,1)} %gi_hbm.1, f32[1024,128]{1,0:T(8,128)} %bitcast.6, bf16[256,256]{1,0:T(8,128)(2,1)} %constant.8.clone.move_hbm, bf16[2,256,512]{2,1,0:T(8,128)(2,1)} %constant.9.clone.pair_hbm, ...), custom_call_target="tpu_custom_call" | custom-call | tf_op jit(solution)/shard_map/pallas_call | solution.py:391
  47.2 1.1 %shard_map.87 = (bf16[2,256,512]{2,1,0:T(8,128)(2,1)}, f32[256,128]{1,0:T(8,128)}) custom-call(bf16[1024,256]{1,0:T(8,128)(2,1)S(1)} %get-tuple-element.6.chunk_rows, f32[128,256]{1,0:T(8,128)S(1)} %get-tuple-element.7.total), custom_call_target="tpu_custom_call" | custom-call | tf_op jit(solution)/shard_map/pallas_call | solution.py:431

commit v5 on v4

--- a/solution.py
+++ b/solution.py
@@ -138,9 +138,9 @@
 
 def kernel(
     og_hbm, gi_hbm, flt_hbm, move_hbm, pair_hbm, tab_hbm, tw_hbm,
-    ig_recv, fg_total,
+    ig_out, fg_out,
     og_in, gi_in, flt, move, pair_move, tab, tw,
-    og_send, gi_send0, gi_send1, ig_send, og_recv, gi_recv0, gi_recv1,
+    og_send, gi_send0, gi_send1, ig_send, og_recv, gi_recv0, gi_recv1, ig_recv,
     rows, grad_spec, flt_spec, fg_part, fg_recv,
     in_sem, send_sem, recv_sem, fg_send_sem, fg_recv_sem,
 ):
@@ -344,39 +344,39 @@
     part_copy(1, far).wait()
     part_copy(2, near).wait()
     total = fg_part[3] + fg_recv[2] + fg_recv[1]
-    fg_total[...] = total
+    total = total * (1.0 / 512.0)
+    for half in range(2):
+        for high in range(2):
+            fg_out[pl.ds(2 * half + high, 64, stride=4), :] = total[
+                half * 64 : half * 64 + 64, high * 128 : high * 128 + 128
+            ]
+    row = lax.broadcasted_iota(jnp.int32, (256, 256), 0)
+    col = lax.broadcasted_iota(jnp.int32, (256, 256), 1)
+    chan = row % 64
+    origin = chan // 4 * 16 + row // 128 * 8 + chan % 4 * 2 + row // 64 % 2
+    back = jnp.where(origin == col, 1.0, 0.0).astype(BF16)
     wait_all(ig_recv, recv_sem, 3)
+    for at in range(4):
+        turned = dot(back, ig_recv[256 * at : 256 * at + 256, :]).astype(BF16)
+        for seq in range(2):
+            for half in range(2):
+                start = seq * 128 + half * 64
+                ig_out[seq, 64 * at : 64 * at + 64, half * 256 : half * 256 + 256] = turned[
+                    start : start + 64
+                ]
     wait_all(og_send, send_sem, 0)
     wait_all(gi_send0, send_sem, 1)
     wait_all(gi_send1, send_sem, 2)
     wait_all(ig_send, send_sem, 3)
 
 
-def finish(chunk_rows, total, ig_hbm, fg_hbm, ig_out, fg_out, sem):
-    scaled = total[...] * (1.0 / 512.0)
-    for half in range(2):
-        for high in range(2):
-            fg_out[pl.ds(2 * half + high, 64, stride=4), :] = scaled[
-                half * 64 : half * 64 + 64, high * 128 : high * 128 + 128
-            ]
-    copies = [pltpu.make_async_copy(fg_out, fg_hbm, sem.at[4])]
-    copies[0].start()
-    row = lax.broadcasted_iota(jnp.int32, (256, 256), 0)
-    col = lax.broadcasted_iota(jnp.int32, (256, 256), 1)
-    chan = row % 64
-    source = chan // 4 * 16 + row // 128 * 8 + chan % 4 * 2 + row // 64 % 2
-    move = jnp.where(source == col, 1.0, 0.0).astype(BF16)
-    for at in range(4):
-        turned = dot(move, chunk_rows[256 * at : 256 * at + 256, :]).astype(BF16)
-        chans = pl.ds(64 * at, 64)
-        for seq in range(2):
-            for half in range(2):
-                start = seq * 128 + half * 64
-                ig_out[seq, chans, half * 256 : half * 256 + 256] = turned[start : start + 64]
-        copies.append(
-            pltpu.make_async_copy(ig_out.at[:, chans, :], ig_hbm.at[:, chans, :], sem.at[at])
-        )
-        copies[-1].start()
+def write_out(ig, fg, ig_hbm, fg_hbm, sem):
+    copies = [
+        pltpu.make_async_copy(ig, ig_hbm, sem.at[0]),
+        pltpu.make_async_copy(fg, fg_hbm, sem.at[1]),
+    ]
+    for copy in copies:
+        copy.start()
     for copy in copies:
         copy.wait()
 
@@ -388,11 +388,11 @@
     vmem = pl.BlockSpec(memory_space=pltpu.VMEM)
     chunks = pltpu.VMEM((CTX * ROWS, 256), BF16)
     pair_chunks = pltpu.VMEM((CTX * ROWS, 128), BF16)
-    chunk_rows, total = pl.pallas_call(
+    input_part, filter_part = pl.pallas_call(
         kernel,
         out_shape=(
-            jax.ShapeDtypeStruct((CTX * ROWS, 256), BF16),
-            jax.ShapeDtypeStruct((128, 256), F32),
+            jax.ShapeDtypeStruct((2, 256, 512), BF16),
+            jax.ShapeDtypeStruct((256, 128), F32),
         ),
         in_specs=[hbm] * 7,
         out_specs=(vmem, vmem),
@@ -404,7 +404,7 @@
             pltpu.VMEM((2, 256, 512), BF16),
             pltpu.VMEM((7, 256, 256), BF16),
             pltpu.VMEM((128, 768), F32),
-            chunks, pair_chunks, pair_chunks, chunks, chunks, pair_chunks, pair_chunks,
+            chunks, pair_chunks, pair_chunks, chunks, chunks, pair_chunks, pair_chunks, chunks,
             chunks,
             pltpu.VMEM((8, 256, 256), F32),
             pltpu.VMEM((4, 256, 256), F32),
@@ -429,7 +429,7 @@
         )
     )
     input_grad, filter_grad = pl.pallas_call(
-        finish,
+        write_out,
         out_shape=(
             jax.ShapeDtypeStruct((2, 256, 512), BF16),
             jax.ShapeDtypeStruct((256, 128), F32),
@@ -437,12 +437,10 @@
         in_specs=[vmem, vmem],
         out_specs=(pl.BlockSpec(memory_space=pl.ANY),) * 2,
         scratch_shapes=[
-            pltpu.VMEM((2, 256, 512), BF16),
-            pltpu.VMEM((256, 128), F32),
-            pltpu.SemaphoreType.DMA((5,)),
+            pltpu.SemaphoreType.DMA((2,)),
         ],
         compiler_params=pltpu.CompilerParams(vmem_limit_bytes=16 * 2**20),
-    )(chunk_rows, total)
+    )(input_part, filter_part)
     return input_grad, filter_grad.reshape(1, 32768)
 
 

time: 48.5 us -> 48.5 us (level)
  no operation moved by 1% of the time
where the time goes in v5:
time: 48.5 us; the launch traced here: 48.3 us
  Pallas kernels  47.7 us (98%)
  between operations  0.64 us (1%)
    pallas_call x1, Pallas kernels, local(): pl.pallas_call(kernel, out_shape=(jax.ShapeDtypeStruct((2, 256, 512), BF1...  46.8 us

profile of v5, /device:TPU:1, one launch (start us, length us, event | category | flops | bytes accessed | tf_op | source)
XLA Modules:
  0.0 48.3 jit_solution(18339044974813313631)
XLA Ops:
  0.6 46.8 %shard_map.86 = (bf16[2,256,512]{2,1,0:T(8,128)(2,1)S(1)}, f32[256,128]{1,0:T(8,128)S(1)}) custom-call(bf16[2,256,512]{2,1,0:T(8,128)(2,1)} %og_hbm.1, bf16[2,256,512]{2,1,0:T(8,128)(2,1)} %gi_hbm.1, f32[1024,128]{1,0:T(8,128)} %bitcast.6, bf16[256,256]{1,0:T(8,128)(2,1)} %constant.8.clone.move_hbm, bf16[2,256,512]{2,1,0:T(8,128)(2,1)} %constant.9.clone.pair_hbm, ...), custom_call_target="tpu_custom_call" | custom-call | tf_op jit(solution)/shard_map/pallas_call | solution.py:391
  47.5 0.8 %shard_map.87 = (bf16[2,256,512]{2,1,0:T(8,128)(2,1)}, f32[256,128]{1,0:T(8,128)}) custom-call(bf16[2,256,512]{2,1,0:T(8,128)(2,1)S(1)} %get-tuple-element.6.ig, f32[256,128]{1,0:T(8,128)S(1)} %get-tuple-element.7.fg), custom_call_target="tpu_custom_call" | custom-call | tf_op jit(solution)/shard_map/pallas_call | solution.py:431
